TPU v7x, 128 devices: a whole 4x4x4 slice. The times are simulated.
128 devices in a mesh: passage: 8 (over y_hi, z), list: 16 (over x, y_lo, core).
Axes of the slice: x: 4, y: 4 (y_hi: 2, y_lo: 2; y = y_hi * 2 + y_lo), z: 4, core: 2. Of those that a mesh axis runs over, the one named last changes fastest.
Arguments:
- passages: bfloat16 [65536, 1024], P(('passage', 'list')), may hold values from -6 to 6
- list_ids: int32 [65536], P(('passage', 'list')), may hold values from 0 to 65535, as said below
- old_centroids: float32 [65536, 1024], P(('passage', 'list')), may hold values from -6 to 6
- rotation: float32 [1024, 1024], replicated, may hold values from -0.1875 to 0.1875
Outputs:
- rotated: bfloat16 [65536, 1024], P(('passage', 'list'))
- centroids: float32 [65536, 1024], P(('passage', 'list'))
Inputs may be any that keep to these rules, and one draw needn't show every extreme that they name: `list_ids`: on each device the ids of its 512 passages never fall. The lists o * 512 to (o + 1) * 512 - 1 belong to owner o, the device of index o along passage+list. At most 8 passages of one device fall in one owner's lists, and in every draw some owners take exactly 8 from every device.
All inputs are finite; a program needn't handle non-finite values.
Results may differ from a plain program's by a relative error of at most 0.001.
Values may be sent and summed in bfloat16 or wider, within the bound.
A program may use at most 64 MiB of HBM per device.

v0:
```python
import jax
import jax.numpy as jnp
from jax import lax
from jax.sharding import PartitionSpec as P


def split_up(array, dim, count):
    before, after = (array.shape[:dim], array.shape[dim + 1 :])
    return jnp.moveaxis(array.reshape(*before, count, -1, *after), dim, 0)


def in_order(parts, dim):
    parts = jnp.moveaxis(parts, 0, dim)
    dims = parts.shape
    return parts.reshape(*dims[:dim], dims[dim] * dims[dim + 1], *dims[dim + 2 :])


def joined_exchange(array, axis, axes, splits, concats):
    sizes = [lax.axis_size(a) for a in axes]
    parts = split_up(array, splits[0], sizes[0])
    parts = jnp.moveaxis(split_up(parts, splits[1] + 1, sizes[1]), 0, 1)
    inside = parts.shape[2:]
    parts = parts.reshape(-1, *inside)
    parts = lax.all_to_all(parts, axis, split_axis=0, concat_axis=0, tiled=True)
    parts = in_order(parts.reshape(*sizes, *inside), concats[0] + 1)
    return in_order(parts, concats[1])


def shards(passages, list_ids, old_centroids, rotation):
    n_pass = lax.axis_size("passage")
    n_list = lax.axis_size("list")
    devices = n_pass * n_list
    rows, width = passages.shape
    list_dev = old_centroids.shape[0]
    capacity = 2 * rows // devices
    owner_of = list_ids // list_dev
    owner_range = jnp.arange(devices, dtype=jnp.int32)
    loads = jnp.sum((owner_of[:, None] == owner_range[None, :]).astype(jnp.int32), axis=0)
    starts = jnp.cumsum(loads) - loads
    slot_range = jnp.arange(capacity, dtype=jnp.int32)
    source_row = starts[:, None] + slot_range[None, :]
    filled = slot_range[None, :] < loads[:, None]
    safe_row = jnp.clip(source_row, 0, rows - 1)
    outgoing = jnp.where(filled[:, :, None], passages[safe_row], jnp.zeros((), jnp.bfloat16))
    local_ids = jnp.where(filled, list_ids[safe_row] % list_dev, list_dev)
    got_rows, got_ids = (
        joined_exchange(
            outgoing.reshape(n_pass, n_list, capacity, width),
            ("passage", "list"),
            ("passage", "list"),
            (0, 1),
            (0, 1),
        ),
        joined_exchange(
            local_ids.reshape(n_pass, n_list, capacity),
            ("passage", "list"),
            ("passage", "list"),
            (0, 1),
            (0, 1),
        ),
    )
    flat_rows = got_rows.reshape(devices * capacity, width)
    flat_ids = got_ids.reshape(devices * capacity)
    list_range = jnp.arange(list_dev, dtype=jnp.int32)
    member = list_range[:, None] == flat_ids[None, :]
    sums = jnp.dot(member.astype(jnp.bfloat16), flat_rows, preferred_element_type=jnp.float32)
    tally = jnp.sum(member.astype(jnp.float32), axis=1)
    centroids = (sums + old_centroids) / (tally[:, None] + 1.0)
    safe_ids = jnp.clip(flat_ids, 0, list_dev - 1)
    back_index = owner_of * capacity + (jnp.arange(rows, dtype=jnp.int32) - starts[owner_of])
    residual = flat_rows.astype(jnp.float32) - jnp.take(centroids, safe_ids, axis=0)
    turned = jnp.dot(
        residual, rotation, preferred_element_type=jnp.float32, precision=lax.Precision.HIGHEST
    )
    turned = turned.astype(jnp.bfloat16).reshape(devices, capacity, width)
    returned = lax.all_to_all(turned, ("passage", "list"), split_axis=0, concat_axis=0, tiled=True)
    rotated = jnp.take(returned.reshape(devices * capacity, width), back_index, axis=0)
    return (rotated, centroids)


def solution(mesh):
    in_specs = (
        P(("passage", "list"), None),
        P(("passage", "list")),
        P(("passage", "list"), None),
        P(),
    )
    out_specs = (P(("passage", "list"), None), P(("passage", "list"), None))
    return jax.shard_map(shards, mesh=mesh, in_specs=in_specs, out_specs=out_specs, check_vma=False)
```

profile of v0, /device:TPU:1, one launch (start us, length us, event | category | flops | bytes accessed | tf_op | source)
XLA Modules:
  0.0 135.1 jit_solution(8592100257078591499)
XLA Ops:
  0.6 0.0 copy-start
  0.6 0.0 copy-start.1
  0.7 0.8 compare_select_fusion.4
  1.4 0.1 convert_reduce_fusion.1
  1.6 0.1 copy.11
  1.7 0.2 reduce-window.7
  1.9 0.1 reduce
  2.0 0.1 compare_select_fusion
  2.1 0.1 reshape.235
  2.2 0.0 copy-done.1
  2.2 6.9 %gather_fusion.2 = s32[1024]{0:T(1024)S(1)} fusion(s32[512]{0:T(512)S(1)} %copy-done.1, s32[1024]{0:T(1024)S(1)} %broadcast_clamp_fusion.2), kind=kCustom, calls=%fused_computation.2 | custom fusion | bytes 12288 | tf_op jit(solution)/shard_map/gather | solution.py:45
  9.1 0.1 gather.25
  9.2 0.7 fusion.15
  9.9 11.5 %all-to-all-start.1 = ((s32[128,1,1,8]{3,2,1,0:T(1,128)}), s32[128,1,1,8]{3,2,1,0:T(1,128)S(1)}, u32[]{:S(2)}, u32[]{:S(2)}) async-start(s32[128,1,1,8]{3,2,1,0:T(1,128)} %bitcast.8), calls=%async_computation.1 | async-start | bytes 131072 | tf_op jit(solution)/shard_map/all_to_all | solution.py:24
  21.4 0.1 iota_compare_fusion.6
  21.5 0.0 copy-done
  21.5 4.1 %gather_fusion.1 = bf16[1024,1024]{1,0:T(8,128)(2,1)S(1)} fusion(bf16[512,1024]{1,0:T(8,128)(2,1)S(1)} %copy-done, s32[1024]{0:T(1024)S(1)} %broadcast_clamp_fusion.2), kind=kCustom, calls=%fused_computation.1 | custom fusion | bytes 4198400 | tf_op jit(solution)/shard_map/gather | solution.py:44
  25.6 1.5 %bitcast_select_fusion = bf16[128,1,1,8,1024]{4,3,2,1,0:T(8,128)(2,1)} fusion(bf16[1024,1024]{1,0:T(8,128)(2,1)S(1)} %gather_fusion.1, pred[128,8]{1,0:T(8,128)(4,1)S(1)} %iota_compare_fusion.6), kind=kLoop, calls=%fused_computation.9 | loop fusion | flops 1048576 | bytes 4195328 | tf_op jit(solution)/shard_map/jit(_where)/select_n | solution.py:44
  27.1 3.8 %all-to-all-done.1 = s32[128,1,1,8]{3,2,1,0:T(1,128)S(1)} async-done(((s32[128,1,1,8]{3,2,1,0:T(1,128)}), s32[128,1,1,8]{3,2,1,0:T(1,128)S(1)}, u32[]{:S(2)}, u32[]{:S(2)}) %all-to-all-start.1) | async-done | bytes 4128 | tf_op jit(solution)/shard_map/all_to_all | solution.py:24
  30.9 6.4 %all-to-all-start = ((bf16[128,1,1,8,1024]{4,3,2,1,0:T(8,128)(2,1)}), bf16[128,1,1,8,1024]{4,3,2,1,0:T(8,128)(2,1)}, u32[]{:S(2)}, u32[]{:S(2)}) async-start(bf16[128,1,1,8,1024]{4,3,2,1,0:T(8,128)(2,1)} %bitcast_select_fusion), calls=%async_computation | async-start | bytes 4194304 | tf_op jit(solution)/shard_map/all_to_all | solution.py:24
  37.3 0.1 reshape_reshape.7
  37.5 0.1 min.28
  37.6 0.3 convert_reduce_fusion
  37.9 29.2 %all-to-all-done = bf16[128,1,1,8,1024]{4,3,2,1,0:T(8,128)(2,1)} async-done(((bf16[128,1,1,8,1024]{4,3,2,1,0:T(8,128)(2,1)}), bf16[128,1,1,8,1024]{4,3,2,1,0:T(8,128)(2,1)}, u32[]{:S(2)}, u32[]{:S(2)}) %all-to-all-start) | async-done | bytes 2097184 | tf_op jit(solution)/shard_map/all_to_all | solution.py:24
  67.1 3.5 %add_divide_fusion = f32[512,1024]{1,0:T(8,128)S(1)} fusion(f32[512,1024]{1,0:T(8,128)} %param.6, bf16[128,1,1,8,1024]{4,3,2,1,0:T(8,128)(2,1)} %all-to-all-done, f32[512]{0:T(512)S(1)} %broadcast_add_fusion, s32[1024]{0:T(1024)S(1)} %reshape_reshape.7), kind=kOutput, calls=%fused_computation.16 | convolution fusion | flops 1075314688 | bytes 6297600 | tf_op jit(solution)/shard_map/dot_general | solution.py:66
  70.6 0.0 copy-start.2
  70.6 5.4 %gather_fusion.3 = f32[1024,1024]{1,0:T(8,128)} fusion(f32[512,1024]{1,0:T(8,128)S(1)} %add_divide_fusion, s32[1024]{0:T(1024)S(1)} %broadcast_clamp_fusion.1), kind=kCustom, calls=%fused_computation.3 | custom fusion | bytes 8392704 | tf_op jit(solution)/shard_map/jit(_take)/gather | solution.py:71
  76.1 0.0 copy-done.2
  76.1 18.4 %convert_bitcast_fusion = bf16[128,8,1024]{2,1,0:T(8,128)(2,1)} fusion(f32[1024,1024]{1,0:T(8,128)} %param.7, f32[1024,1024]{1,0:T(8,128)} %gather_fusion.3, bf16[128,1,1,8,1024]{4,3,2,1,0:T(8,128)(2,1)} %all-to-all-done, pred[1024]{0:T(1024)(128)(4,1)S(1)} %compare_and_fusion), kind=kOutput, calls=%fused_computation.13 | convolution fusion | flops 12889096192 | bytes 12583936 | tf_op jit(solution)/shard_map/dot_general | solution.py:72
  94.4 5.4 %all-to-all-start.2 = ((bf16[128,8,1024]{2,1,0:T(8,128)(2,1)}), bf16[128,8,1024]{2,1,0:T(8,128)(2,1)S(1)}, u32[]{:S(2)}, u32[]{:S(2)}) async-start(bf16[128,8,1024]{2,1,0:T(8,128)(2,1)} %convert_bitcast_fusion), calls=%async_computation.2 | async-start | bytes 4194304 | tf_op jit(solution)/shard_map/all_to_all | solution.py:76
  99.9 3.3 %gather_fusion = s32[512]{0:T(512)S(1)} fusion(s32[128]{0:T(128)S(1)} %sub.20, s32[1024]{0:T(1024)S(1)} %pad_clamp_fusion.1), kind=kCustom, calls=%fused_computation | custom fusion | bytes 6144 | tf_op jit(solution)/shard_map/gather | solution.py:70
  103.2 26.7 %all-to-all-done.2 = bf16[128,8,1024]{2,1,0:T(8,128)(2,1)S(1)} async-done(((bf16[128,8,1024]{2,1,0:T(8,128)(2,1)}), bf16[128,8,1024]{2,1,0:T(8,128)(2,1)S(1)}, u32[]{:S(2)}, u32[]{:S(2)}) %all-to-all-start.2) | async-done | bytes 2097184 | tf_op jit(solution)/shard_map/all_to_all | solution.py:76
  130.0 2.8 %gather_fusion.4 = bf16[512,1024]{1,0:T(8,128)(2,1)} fusion(bf16[1024,1024]{1,0:T(8,128)(2,1)S(1)} %bitcast.47, s32[1024]{0:T(1024)S(1)} %pad_clamp_fusion), kind=kCustom, calls=%fused_computation.4 | custom fusion | bytes 2099200 | tf_op jit(solution)/shard_map/jit(_take)/gather | solution.py:77
  132.8 2.4 %broadcast_select_fusion = bf16[512,1024]{1,0:T(8,128)(2,1)} fusion(bf16[512,1024]{1,0:T(8,128)(2,1)} %gather_fusion.4, pred[512]{0:T(512)(128)(4,1)S(1)} %get-tuple-element.2), kind=kLoop, calls=%fused_computation.20 | loop fusion | flops 524288 | bytes 2097664 | tf_op jit(solution)/shard_map/jit(_take)/select_n | solution.py:77
  (10 shorter events, 0.1 us)
Async XLA Ops:
  0.6 20.9 %copy-start = (bf16[512,1024]{1,0:T(8,128)(2,1)S(1)}, bf16[512,1024]{1,0:T(8,128)(2,1)}, u32[]{:S(2)}) copy-start(bf16[512,1024]{1,0:T(8,128)(2,1)} %param.4) | copy-start | bytes 3145732
  0.6 1.6 %copy-start.1 = (s32[512]{0:T(512)S(1)}, s32[512]{0:T(512)}, u32[]{:S(2)}) copy-start(s32[512]{0:T(512)} %param.5) | copy-start | bytes 6148
  9.9 21.0 %all-to-all-start.1 = ((s32[128,1,1,8]{3,2,1,0:T(1,128)}), s32[128,1,1,8]{3,2,1,0:T(1,128)S(1)}, u32[]{:S(2)}, u32[]{:S(2)}) async-start(s32[128,1,1,8]{3,2,1,0:T(1,128)} %bitcast.8), calls=%async_computation.1 | async-start | bytes 131072 | tf_op jit(solution)/shard_map/all_to_all | solution.py:24
  30.9 36.2 %all-to-all-start = ((bf16[128,1,1,8,1024]{4,3,2,1,0:T(8,128)(2,1)}), bf16[128,1,1,8,1024]{4,3,2,1,0:T(8,128)(2,1)}, u32[]{:S(2)}, u32[]{:S(2)}) async-start(bf16[128,1,1,8,1024]{4,3,2,1,0:T(8,128)(2,1)} %bitcast_select_fusion), calls=%async_computation | async-start | bytes 4194304 | tf_op jit(solution)/shard_map/all_to_all | solution.py:24
  70.6 5.4 %copy-start.2 = (f32[512,1024]{1,0:T(8,128)}, f32[512,1024]{1,0:T(8,128)S(1)}, u32[]{:S(2)}) copy-start(f32[512,1024]{1,0:T(8,128)S(1)} %add_divide_fusion) | copy-start | bytes 6291460
  94.4 35.6 %all-to-all-start.2 = ((bf16[128,8,1024]{2,1,0:T(8,128)(2,1)}), bf16[128,8,1024]{2,1,0:T(8,128)(2,1)S(1)}, u32[]{:S(2)}, u32[]{:S(2)}) async-start(bf16[128,8,1024]{2,1,0:T(8,128)(2,1)} %convert_bitcast_fusion), calls=%async_computation.2 | async-start | bytes 4194304 | tf_op jit(solution)/shard_map/all_to_all | solution.py:76
where the time goes:
time: 135 us
  waiting for transfers between devices  59.7 us (44%)
  starting transfers between devices  23.4 us (17%)
  local copies, waits for them, and re-layouts  23 us (17%)
  matrix products  21.8 us (16%)
  other arithmetic  6.37 us (5%)
    all_to_all x2, waiting for transfers between devices, joined_exchange(): parts = lax.all_to_all(parts, axis, split_axis=0, concat_axis=0, tiled=True)  33 us
    all_to_all x1, waiting for transfers between devices, shards(): lax.all_to_all(turned, ('passage', 'list'), split_axis=0, concat_axis=0,...  26.7 us
    dot_general x1, matrix products, shards(): jnp.dot(residual, rotation, preferred_element_type=jnp.float32, precision...  18.4 us
    all_to_all x2, starting transfers between devices, joined_exchange(): parts = lax.all_to_all(parts, axis, split_axis=0, concat_axis=0, tiled=True)  17.9 us
    gather x2, local copies, waits for them, and re-layouts, shards(): local_ids = jnp.where(filled, list_ids[safe_row] % list_dev, list_dev)  6.94 us
    gather x1, local copies, waits for them, and re-layouts, shards(): jnp.take(centroids, safe_ids, axis=0)  5.43 us
    all_to_all x1, starting transfers between devices, shards(): lax.all_to_all(turned, ('passage', 'list'), split_axis=0, concat_axis=0,...  5.42 us
    gather x1, local copies, waits for them, and re-layouts, shards(): passages[safe_row]  4.07 us
  transfers between devices with their start and end apart: 3, of which 3 were waited for; matrix products, arithmetic and copies ran while one was open for 7% of the time, Pallas kernels for 0%

commit v1 on v0

v1 whole, which is shorter than its diff:
```python
import jax
import jax.numpy as jnp
from jax import lax
from jax.experimental import pallas as pl
from jax.experimental.pallas import tpu as pltpu
from jax.sharding import PartitionSpec as P

NP, NL = 8, 16
DEV = NP * NL
CAP = 8
ROWS = 512
LISTS = 512
D = 1024
BLK = NL * CAP
TILE = 256
MESH = pl.DeviceIdType.MESH
F32, BF16, I32 = jnp.float32, jnp.bfloat16, jnp.int32


def dot(a, b):
    return jnp.dot(a, b, preferred_element_type=F32)


def iota(shape, dim):
    return lax.broadcasted_iota(I32, shape, dim)


def far_first(digit):
    return (2 - digit) + 3 * (digit // 2) - 2 * (digit // 3)


def device_at(x, y, z, core):
    return ((y // 2) * 4 + z, x * 4 + (y % 2) * 2 + core)


def whole(ref, sem):
    pltpu.make_async_copy(ref, ref, sem).wait()


def kernel(
    ids_ref, pass_ref, old_hbm, rot_hbm, out_ref, cent_hbm,
    old, rot, rot_hi, rot_lo, send1, recv1, send2, recv2,
    cent, cent_hi, cent_lo, res_hi, res_lo, member, member_t, unpack,
    id1_s, id1_r, id2_s, id2_r,
    sem_send, sem_recv, sem_id, sem_local, sem_bar,
):
    p, l = lax.axis_index("passage"), lax.axis_index("list")
    me = p * NL + l
    x, y, z = l // 4, (p // 4) * 2 + (l // 2) % 2, p % 4

    barrier = pltpu.get_barrier_semaphore()

    def greet_row(k, _):
        pl.semaphore_signal(barrier, inc=1, device_id=(p, (l + k) % NL), device_id_type=MESH)
        return 0

    def greet_column(k, _):
        pl.semaphore_signal(barrier, inc=1, device_id=((p + k) % NP, l), device_id_type=MESH)
        return 0

    lax.fori_loop(1, NP, greet_column, 0)
    lax.fori_loop(1, NL, greet_row, 0)

    load_old = pltpu.make_async_copy(old_hbm, old, sem_local.at[0])
    load_rot = pltpu.make_async_copy(rot_hbm, rot, sem_local.at[1])
    load_rot.start()
    load_old.start()

    ids_row = ids_ref[...].astype(F32)
    eye = iota((ROWS, ROWS), 0) == iota((ROWS, ROWS), 1)
    ids_col = jnp.sum(jnp.where(eye, ids_row, 0.0), axis=1, keepdims=True)
    own_row = jnp.floor(ids_row * (1.0 / LISTS))
    own_col = jnp.floor(ids_col * (1.0 / LISTS))
    before_row = jnp.sum(jnp.where(own_col < own_row, 1.0, 0.0), axis=0, keepdims=True)
    before_col = jnp.sum(jnp.where(own_row < own_col, 1.0, 0.0), axis=1, keepdims=True)
    slot_row = (own_row * CAP + iota((1, ROWS), 1).astype(F32) - before_row).astype(I32)
    slot_col = (own_col * CAP + iota((ROWS, 1), 0).astype(F32) - before_col).astype(I32)
    mark_col = ids_col - own_col * LISTS + 1.0

    for b in range(NP):
        hit = slot_col == iota((ROWS, BLK), 1) + b * BLK
        id1_s[b] = jnp.sum(jnp.where(hit, mark_col, 0.0), axis=0, keepdims=True).astype(I32)
        unpack[:, b * BLK : (b + 1) * BLK] = jnp.where(hit, 1.0, 0.0).astype(BF16)

    def fill(b, _):
        hit = slot_row == iota((BLK, ROWS), 0) + b * BLK
        rows = dot(jnp.where(hit, 1.0, 0.0).astype(BF16), pass_ref[...])
        send1[pl.ds(b * NL, NL)] = rows.astype(BF16).reshape(NL, CAP, D)
        return 0

    lax.fori_loop(0, NP, fill, 0)

    load_rot.wait()

    def split_rot(i, _):
        s = pl.ds(pl.multiple_of(i * 128, 128), 128)
        full = rot[s, :]
        high = full.astype(BF16)
        rot_hi[s, :] = high
        rot_lo[s, :] = (full - high.astype(F32)).astype(BF16)
        return 0

    lax.fori_loop(0, D // 128, split_rot, 0)

    pl.semaphore_wait(barrier, NP + NL - 2)

    def row_is_in(k, _):
        pl.semaphore_signal(sem_bar, inc=1, device_id=((p + k) % NP, l), device_id_type=MESH)
        return 0

    lax.fori_loop(1, NP, row_is_in, 0)

    def id_hop1(k, _):
        other = (p + k) % NP
        pltpu.make_async_remote_copy(
            src_ref=id1_s.at[other], dst_ref=id1_r.at[p], send_sem=sem_id.at[0], recv_sem=sem_id.at[1],
            device_id=(other, l), device_id_type=MESH,
        ).start()
        return 0

    lax.fori_loop(1, NP, id_hop1, 0)
    pltpu.make_async_copy(id1_s.at[p], id1_r.at[p], sem_id.at[1]).start()
    pl.semaphore_wait(sem_bar, NP - 1)

    def route(k, _):
        core, turn, a, b = k // 64, (k // 16) % 4, (k // 4) % 4, k % 4
        c = (turn + a + b) % 4
        dev = device_at((x + far_first(a)) % 4, (y + far_first(b)) % 4, (z + far_first(c)) % 4, core)
        there = dev[0] * NL + dev[1]

        @pl.when(there != me)
        def _():
            pltpu.make_async_remote_copy(
                src_ref=send1.at[there], dst_ref=recv1.at[me], send_sem=sem_send.at[0], recv_sem=sem_recv.at[0],
                device_id=dev, device_id_type=MESH,
            ).start()

        return 0

    lax.fori_loop(0, DEV // 2, route, 0)
    pltpu.make_async_copy(send1.at[me], recv1.at[me], sem_recv.at[0]).start()

    whole(id1_r, sem_id.at[1])
    lane = iota((NP, BLK), 1)
    mine = (lane >= l * CAP) & (lane < l * CAP + CAP)
    got = id1_r[...].reshape(NP, BLK)
    for k in range(NL):
        turned = pltpu.roll(got, lax.rem(l - k + NL, NL) * CAP, 1)
        id2_s[k] = jnp.where(mine, turned, 0)

    def id_hop2(k, _):
        other = (l + k) % NL
        pltpu.make_async_remote_copy(
            src_ref=id2_s.at[other], dst_ref=id2_r.at[l], send_sem=sem_id.at[2], recv_sem=sem_id.at[3],
            device_id=(p, other), device_id_type=MESH,
        ).start()
        return 0

    lax.fori_loop(1, NL, id_hop2, 0)
    pltpu.make_async_copy(id2_s.at[l], id2_r.at[l], sem_id.at[3]).start()

    lax.fori_loop(DEV // 2, DEV, route, 0)

    whole(id2_r, sem_id.at[3])
    marks = jnp.sum(id2_r[...].astype(F32), axis=0)
    eye = iota((BLK, BLK), 0) == iota((BLK, BLK), 1)
    tally = jnp.zeros((LISTS, 1), F32)
    for b in range(NP):
        row = marks[b : b + 1, :]
        hit = jnp.where(iota((LISTS, BLK), 0) + 1 == row.astype(I32), 1.0, 0.0)
        member[:, b * BLK : (b + 1) * BLK] = hit.astype(BF16)
        tally = tally + jnp.sum(hit, axis=1, keepdims=True)
        col = jnp.sum(jnp.where(eye, row, 0.0), axis=1, keepdims=True).astype(I32)
        hit = jnp.where(iota((BLK, LISTS), 1) + 1 == col, 1.0, 0.0)
        member_t[b * BLK : (b + 1) * BLK, :] = hit.astype(BF16)
    load_old.wait()
    tally = tally + 1.0

    whole(recv1, sem_recv.at[0])
    for n in range(D // TILE):
        s = slice(n * TILE, (n + 1) * TILE)
        sums = dot(member[...], recv1[:, :, s].reshape(DEV * CAP, TILE))
        mean = (sums + old[:, s]) / tally
        high = mean.astype(BF16)
        cent[:, s] = mean
        cent_hi[:, s] = high
        cent_lo[:, s] = (mean - high.astype(F32)).astype(BF16)
    store_cent = pltpu.make_async_copy(cent, cent_hbm, sem_local.at[2])
    store_cent.start()

    def chunk(i, _):
        y_hi = (p // 4 + 1 + i // 2) % 2
        z_a = (z + 2 + i % 2) % 4
        z_b = (z + 1 + 3 * (i % 2)) % 4
        blocks = (y_hi * 4 + z_a, y_hi * 4 + z_b)
        for h, blk in enumerate(blocks):
            half = slice(h * BLK, (h + 1) * BLK)
            pick = member_t[pl.ds(pl.multiple_of(blk * BLK, BLK), BLK), :]
            for n in range(D // TILE):
                s = slice(n * TILE, (n + 1) * TILE)
                near = dot(pick, cent_hi[:, s]) + dot(pick, cent_lo[:, s])
                rows = recv1[pl.ds(blk * NL, NL), :, s].reshape(BLK, TILE).astype(F32)
                res = rows - near
                high = res.astype(BF16)
                res_hi[half, s] = high
                res_lo[half, s] = (res - high.astype(F32)).astype(BF16)
        for n in range(D // TILE):
            s = slice(n * TILE, (n + 1) * TILE)
            turned = dot(res_hi[...], rot_hi[:, s]) + dot(res_hi[...], rot_lo[:, s]) + dot(res_lo[...], rot_hi[:, s])
            turned = turned.astype(BF16)
            for h, blk in enumerate(blocks):
                send2[pl.ds(blk * NL, NL), :, s] = turned[h * BLK : (h + 1) * BLK].reshape(NL, CAP, TILE)

        def give_back(k, _):
            core, h, a, b = k // 16, (k // 8) % 2, (k // 2) % 4, k % 2
            z_to = z_a * (1 - h) + z_b * h
            there_p = y_hi * 4 + z_to
            there_l = ((x + far_first(a)) % 4) * 4 + ((l // 2 + 1 + b) % 2) * 2 + core
            there = there_p * NL + there_l

            @pl.when(there != me)
            def _():
                pltpu.make_async_remote_copy(
                    src_ref=send2.at[there], dst_ref=recv2.at[me], send_sem=sem_send.at[1], recv_sem=sem_recv.at[1],
                    device_id=(there_p, there_l), device_id_type=MESH,
                ).start()

            return 0

        lax.fori_loop(0, 2 * NL, give_back, 0)
        return 0

    lax.fori_loop(0, NP // 2, chunk, 0)
    pltpu.make_async_copy(send2.at[me], recv2.at[me], sem_recv.at[1]).start()

    whole(recv2, sem_recv.at[1])
    for n in range(D // TILE):
        s = slice(n * TILE, (n + 1) * TILE)
        out_ref[:, s] = dot(unpack[...], recv2[:, :, s].reshape(DEV * CAP, TILE)).astype(BF16)

    store_cent.wait()
    whole(send1.at[pl.ds(0, DEV - 1)], sem_send.at[0])
    whole(send2.at[pl.ds(0, DEV - 1)], sem_send.at[1])
    whole(id1_s.at[pl.ds(0, NP - 1)], sem_id.at[0])
    whole(id2_s.at[pl.ds(0, NL - 1)], sem_id.at[2])


def shards(passages, list_ids, old_centroids, rotation):
    vmem = pl.BlockSpec(memory_space=pltpu.VMEM)
    hbm = pl.BlockSpec(memory_space=pl.ANY)
    slots = pltpu.VMEM((DEV, CAP, D), BF16)
    return pl.pallas_call(
        kernel,
        out_shape=(
            jax.ShapeDtypeStruct((ROWS, D), BF16),
            jax.ShapeDtypeStruct((LISTS, D), F32),
        ),
        in_specs=[vmem, vmem, hbm, hbm],
        out_specs=(vmem, hbm),
        scratch_shapes=[
            pltpu.VMEM((LISTS, D), F32),
            pltpu.VMEM((D, D), F32),
            pltpu.VMEM((D, D), BF16),
            pltpu.VMEM((D, D), BF16),
            slots, slots, slots, slots,
            pltpu.VMEM((LISTS, D), F32),
            pltpu.VMEM((LISTS, D), BF16),
            pltpu.VMEM((LISTS, D), BF16),
            pltpu.VMEM((2 * BLK, D), BF16),
            pltpu.VMEM((2 * BLK, D), BF16),
            pltpu.VMEM((LISTS, DEV * CAP), BF16),
            pltpu.VMEM((DEV * CAP, LISTS), BF16),
            pltpu.VMEM((ROWS, DEV * CAP), BF16),
            pltpu.VMEM((NP, 1, BLK), I32),
            pltpu.VMEM((NP, 1, BLK), I32),
            pltpu.VMEM((NL, NP, BLK), I32),
            pltpu.VMEM((NL, NP, BLK), I32),
            pltpu.SemaphoreType.DMA((2,)),
            pltpu.SemaphoreType.DMA((2,)),
            pltpu.SemaphoreType.DMA((4,)),
            pltpu.SemaphoreType.DMA((3,)),
            pltpu.SemaphoreType.REGULAR,
        ],
        compiler_params=pltpu.CompilerParams(
            collective_id=0, has_side_effects=True, vmem_limit_bytes=48 << 20
        ),
        cost_estimate=pl.CostEstimate(flops=14 << 30, bytes_accessed=10 << 20, transcendentals=0),
    )(list_ids.reshape(1, ROWS), passages, old_centroids, rotation)


def solution(mesh):
    split = P(("passage", "list"), None)
    return jax.shard_map(
        shards,
        mesh=mesh,
        in_specs=(split, P(("passage", "list")), split, P()),
        out_specs=(split, split),
        check_vma=False,
    )
```

time: 135 us -> 70.5 us (0.52)
  Pallas kernels: 0 us -> 65.4 us
  waiting for transfers between devices: 59.7 us -> 0 us
  starting transfers between devices: 23.4 us -> 0 us
  matrix products: 21.8 us -> 0 us
  local copies, waits for them, and re-layouts: 23 us -> 4.19 us
  other arithmetic: 6.37 us -> 0 us
    pallas_call x0 -> x1, Pallas kernels: none -> 65.4 us  [shards(): pl.pallas_call(kernel, out_shape=(jax.ShapeDtypeStruct((ROWS, D), BF16),...]
    all_to_all x3 -> x0, waiting for transfers between devices: 59.7 us -> none  [the longest x2 33 us: joined_exchange(): parts = lax.all_to_all(parts, axis, split_axis=0, concat_axis=0, tiled=True)]
    all_to_all x3 -> x0, starting transfers between devices: 23.4 us -> none  [the longest x2 17.9 us: joined_exchange(): parts = lax.all_to_all(parts, axis, split_axis=0, concat_axis=0, tiled=True)]
    gather x6 -> x0, local copies, waits for them, and re-layouts: 22.6 us -> none  [the longest x2 6.94 us: shards(): local_ids = jnp.where(filled, list_ids[safe_row] % list_dev, list_dev)]
    dot_general x2 -> x0, matrix products: 21.8 us -> none  [the longest x1 18.4 us: shards(): jnp.dot(residual, rotation, preferred_element_type=jnp.float32, precision...]
    select_n x6 -> x0, other arithmetic: 5.51 us -> none  [the longest x1 2.36 us: shards(): jnp.take(returned.reshape(devices * capacity, width), back_index, axis=0)]
    unnamed x6, local copies, waits for them, and re-layouts: 0.02 us -> 4.19 us
  transfers between devices with their start and end apart: 3 -> 0, of which waited for: 3 -> 0; matrix products, arithmetic and copies ran while one was open for 7% -> 0% of each run, Pallas kernels for 0% -> 0%
where the time goes in v1:
time: 70.5 us; the launch traced here: 70.3 us
  Pallas kernels  65.4 us (93%)
  local copies, waits for them, and re-layouts  4.19 us (6%)
    pallas_call x1, Pallas kernels, shards(): pl.pallas_call(kernel, out_shape=(jax.ShapeDtypeStruct((ROWS, D), BF16),...  65.4 us
    unnamed x6, local copies, waits for them, and re-layouts  4.19 us

profile of v1, /device:TPU:1, one launch (start us, length us, event | category | flops | bytes accessed | tf_op | source)
XLA Modules:
  0.0 70.3 jit_solution(10615109136164356031)
XLA Ops:
  0.6 0.0 copy-start
  0.6 1.2 %copy-done = bf16[512,1024]{1,0:T(8,128)(2,1)S(1)} copy-done((bf16[512,1024]{1,0:T(8,128)(2,1)S(1)}, bf16[512,1024]{1,0:T(8,128)(2,1)}, u32[]{:S(2)}) %copy-start) | copy-done | bytes 1048600
  1.9 0.0 copy-start.1
  1.9 0.7 copy-done.1
  2.5 65.4 %shard_map.59 = (bf16[512,1024]{1,0:T(8,128)(2,1)S(1)}, f32[512,1024]{1,0:T(8,128)S(1)}) custom-call(s32[1,512]{1,0:T(1,128)S(1)} %bitcast.1, bf16[512,1024]{1,0:T(8,128)(2,1)S(1)} %copy-done, f32[512,1024]{1,0:T(8,128)} %old_hbm.1, f32[1024,1024]{1,0:T(8,128)} %rot_hbm.1), custom_call_target="tpu_custom_call" | custom-call | flops 15032385536 | bytes 10485760 | tf_op jit(solution)/shard_map/pallas_call | solution.py:252
  68.0 1.0 %copy.8 = bf16[512,1024]{1,0:T(8,128)(2,1)} copy(bf16[512,1024]{1,0:T(8,128)(2,1)S(1)} %get-tuple-element.4) | data formatting | bytes 2097152
  69.0 1.3 %copy.9 = f32[512,1024]{1,0:T(8,128)} copy(f32[512,1024]{1,0:T(8,128)S(1)} %get-tuple-element.5) | data formatting | bytes 4194304
Async XLA Ops:
  0.6 1.2 %copy-start = (bf16[512,1024]{1,0:T(8,128)(2,1)S(1)}, bf16[512,1024]{1,0:T(8,128)(2,1)}, u32[]{:S(2)}) copy-start(bf16[512,1024]{1,0:T(8,128)(2,1)} %pass_ref.1) | copy-start | bytes 3145732
  1.9 0.7 copy-start.1

commit v2 on v1

v2 whole, which is shorter than its diff:
```python
import jax
import jax.numpy as jnp
from jax import lax
from jax.experimental import pallas as pl
from jax.experimental.pallas import tpu as pltpu
from jax.sharding import PartitionSpec as P

NP, NL = 8, 16
DEV = NP * NL
CAP = 8
ROWS = 512
LISTS = 512
D = 1024
BLK = NL * CAP
TILE = 256
MESH = pl.DeviceIdType.MESH
F32, BF16, I32 = jnp.float32, jnp.bfloat16, jnp.int32


def dot(a, b):
    return jnp.dot(a, b, preferred_element_type=F32)


def iota(shape, dim):
    return lax.broadcasted_iota(I32, shape, dim)


def wrap(v, n):
    return jnp.where(v >= n, v - n, v)


def steps(offset):
    return sum(min(d, 4 - d) for d in offset)


OFFSETS = sorted(((a, b, c) for a in range(4) for b in range(4) for c in range(4)), key=steps, reverse=True)
HERE = (0, 0, 0)


class Place:
    def __init__(self):
        self.p, self.l = lax.axis_index("passage"), lax.axis_index("list")
        x, self.y_hi = lax.div(self.l, 4), lax.div(self.p, 4)
        z, rest = self.p - 4 * self.y_hi, self.l - 4 * x
        self.y_lo = lax.div(rest, 2)
        self.core = rest - 2 * self.y_lo
        y = 2 * self.y_hi + self.y_lo
        ys = [wrap(y + d, 4) for d in range(4)]
        self.x_part = [4 * wrap(x + d, 4) for d in range(4)]
        self.z_part = [wrap(z + d, 4) for d in range(4)]
        self.hi_part = [jnp.where(v >= 2, 4, 0) for v in ys]
        self.lo_part = [2 * (v - jnp.where(v >= 2, 2, 0)) for v in ys]
        self.me = self.p * NL + self.l

    def at(self, offset, core):
        a, b, c = offset
        return (self.hi_part[b] + self.z_part[c], self.x_part[a] + self.lo_part[b] + core)


def whole(ref, sem):
    pltpu.make_async_copy(ref, ref, sem).wait()


def signal(sem, device):
    pl.semaphore_signal(sem, inc=1, device_id=device, device_id_type=MESH)


def kernel(
    ids_hbm, pass_hbm, old_hbm, rot_hbm, recv2, cent_out, unpack_out,
    ids_ref, pass_ref, old, rot, rot_hi, rot_lo, send1, recv1, send2,
    cent, cent_hi, cent_lo, res_hi, res_lo, member, member_t, unpack,
    id1_s, id1_r, id2_s, id2_r,
    sem_send, sem_recv, sem_id, sem_local, sem_bar,
):
    at = Place()
    p, l, me = at.p, at.l, at.me

    load_ids = pltpu.make_async_copy(ids_hbm, ids_ref, sem_local.at[0])
    load_pass = pltpu.make_async_copy(pass_hbm, pass_ref, sem_local.at[1])
    load_rot = pltpu.make_async_copy(rot_hbm, rot, sem_local.at[2])
    load_old = pltpu.make_async_copy(old_hbm, old, sem_local.at[3])
    load_ids.start()
    load_pass.start()

    barrier = pltpu.get_barrier_semaphore()
    plane = [(0, b, c) for b in (2, 1, 3, 0) for c in (2, 1, 3, 0) if (b, c) != (0, 0)]
    line = [(a, 0, 0) for a in (2, 1, 3)]
    for offset in plane:
        signal(barrier, at.at(offset, at.core))
    for offset in line:
        for core in range(2):
            signal(barrier, at.at(offset, core))
    signal(barrier, at.at(HERE, 1 - at.core))
    load_rot.start()
    load_old.start()

    load_ids.wait()
    ids_row = ids_ref[...].astype(F32)
    eye = iota((ROWS, ROWS), 0) == iota((ROWS, ROWS), 1)
    ids_col = jnp.sum(jnp.where(eye, ids_row, 0.0), axis=1, keepdims=True)
    own_row = jnp.floor(ids_row * (1.0 / LISTS))
    own_col = jnp.floor(ids_col * (1.0 / LISTS))
    before_row = jnp.sum(jnp.where(own_col < own_row, 1.0, 0.0), axis=0, keepdims=True)
    slot_row = (own_row * CAP + iota((1, ROWS), 1).astype(F32) - before_row).astype(I32)

    load_pass.wait()

    def fill(b, _):
        hit = slot_row == iota((BLK, ROWS), 0) + b * BLK
        rows = dot(jnp.where(hit, 1.0, 0.0).astype(BF16), pass_ref[...])
        send1[pl.ds(b * NL, NL)] = rows.astype(BF16).reshape(NL, CAP, D)
        return 0

    lax.fori_loop(0, NP, fill, 0)

    def route(offset, core):
        device = at.at(offset, core)
        pltpu.make_async_remote_copy(
            src_ref=send1.at[device[0] * NL + device[1]], dst_ref=recv1.at[me],
            send_sem=sem_send.at[0], recv_sem=sem_recv.at[0], device_id=device, device_id_type=MESH,
        ).start()

    pl.semaphore_wait(barrier, len(plane) + 2 * len(line) + 1)
    for offset in plane:
        signal(sem_bar, at.at(offset, at.core))
    for offset in plane:
        route(offset, at.core)
    for offset in line:
        for core in range(2):
            route(offset, core)
    route(HERE, 1 - at.core)
    pltpu.make_async_copy(send1.at[me], recv1.at[me], sem_recv.at[0]).start()

    before_col = jnp.sum(jnp.where(own_row < own_col, 1.0, 0.0), axis=1, keepdims=True)
    slot_col = (own_col * CAP + iota((ROWS, 1), 0).astype(F32) - before_col).astype(I32)
    mark_col = ids_col - own_col * LISTS + 1.0
    for b in range(NP):
        hit = slot_col == iota((ROWS, BLK), 1) + b * BLK
        id1_s[b] = jnp.sum(jnp.where(hit, mark_col, 0.0), axis=0, keepdims=True).astype(I32)
        unpack[:, b * BLK : (b + 1) * BLK] = jnp.where(hit, 1.0, 0.0).astype(BF16)
    for b in (2, 0):
        for c in (2, 1, 3, 0):
            if (b, c) != (0, 0):
                device = at.at((0, b, c), at.core)
                pltpu.make_async_remote_copy(
                    src_ref=id1_s.at[device[0]], dst_ref=id1_r.at[p], send_sem=sem_id.at[0], recv_sem=sem_id.at[1],
                    device_id=device, device_id_type=MESH,
                ).start()
    pltpu.make_async_copy(id1_s.at[p], id1_r.at[p], sem_id.at[1]).start()
    store_unpack = pltpu.make_async_copy(unpack, unpack_out, sem_local.at[0])
    store_unpack.start()
    pl.semaphore_wait(sem_bar, len(plane))

    others = [offset for offset in OFFSETS if offset[0] != 0 and offset[1:] != (0, 0)]

    def route_all(core):
        for offset in others:
            route(offset, core)

        @pl.when(at.core != core)
        def _():
            for offset in plane:
                route(offset, core)

    route_all(0)

    whole(id1_r, sem_id.at[1])
    lane = iota((NP, BLK), 1)
    mine = (lane >= l * CAP) & (lane < l * CAP + CAP)
    got = id1_r[...].reshape(NP, BLK)
    for k in range(NL):
        id2_s[k] = jnp.where(mine, pltpu.roll(got, CAP * wrap(l - k + NL, NL), 1), 0)
    for k in range(1, NL):
        other = wrap(l + k, NL)
        pltpu.make_async_remote_copy(
            src_ref=id2_s.at[other], dst_ref=id2_r.at[l], send_sem=sem_id.at[2], recv_sem=sem_id.at[3],
            device_id=(p, other), device_id_type=MESH,
        ).start()
    pltpu.make_async_copy(id2_s.at[l], id2_r.at[l], sem_id.at[3]).start()

    route_all(1)

    load_rot.wait()

    def split_rot(i, _):
        s = pl.ds(pl.multiple_of(i * 128, 128), 128)
        full = rot[s, :]
        high = full.astype(BF16)
        rot_hi[s, :] = high
        rot_lo[s, :] = (full - high.astype(F32)).astype(BF16)
        return 0

    lax.fori_loop(0, D // 128, split_rot, 0)

    whole(id2_r, sem_id.at[3])
    marks = jnp.sum(id2_r[...].astype(F32), axis=0)
    eye = iota((BLK, BLK), 0) == iota((BLK, BLK), 1)
    tally = jnp.zeros((LISTS, 1), F32)
    for b in range(NP):
        row = marks[b : b + 1, :]
        hit = jnp.where(iota((LISTS, BLK), 0) + 1 == row.astype(I32), 1.0, 0.0)
        member[:, b * BLK : (b + 1) * BLK] = hit.astype(BF16)
        tally = tally + jnp.sum(hit, axis=1, keepdims=True)
        col = jnp.sum(jnp.where(eye, row, 0.0), axis=1, keepdims=True).astype(I32)
        hit = jnp.where(iota((BLK, LISTS), 1) + 1 == col, 1.0, 0.0)
        member_t[b * BLK : (b + 1) * BLK, :] = hit.astype(BF16)
    load_old.wait()
    tally = tally + 1.0

    whole(recv1, sem_recv.at[0])
    for n in range(D // TILE):
        s = slice(n * TILE, (n + 1) * TILE)
        sums = dot(member[...], recv1[:, :, s].reshape(DEV * CAP, TILE))
        mean = (sums + old[:, s]) / tally
        high = mean.astype(BF16)
        cent[:, s] = mean
        cent_hi[:, s] = high
        cent_lo[:, s] = (mean - high.astype(F32)).astype(BF16)
    store_cent = pltpu.make_async_copy(cent, cent_out, sem_local.at[1])
    store_cent.start()

    def chunk(i, _):
        far = lax.div(i, 2)
        flip = i - 2 * far
        y_hi = wrap(at.y_hi + 1 + far, 2)
        y_hi = wrap(y_hi, 2)
        z_a = wrap(at.z_part[0] + 2 + flip, 4)
        z_b = wrap(at.z_part[0] + 1 + 3 * flip, 4)
        z_b = wrap(z_b, 4)
        blocks = (y_hi * 4 + z_a, y_hi * 4 + z_b)
        for h, blk in enumerate(blocks):
            half = slice(h * BLK, (h + 1) * BLK)
            pick = member_t[pl.ds(pl.multiple_of(blk * BLK, BLK), BLK), :]
            for n in range(D // TILE):
                s = slice(n * TILE, (n + 1) * TILE)
                near = dot(pick, cent_hi[:, s]) + dot(pick, cent_lo[:, s])
                rows = recv1[pl.ds(blk * NL, NL), :, s].reshape(BLK, TILE).astype(F32)
                res = rows - near
                high = res.astype(BF16)
                res_hi[half, s] = high
                res_lo[half, s] = (res - high.astype(F32)).astype(BF16)
        for n in range(D // TILE):
            s = slice(n * TILE, (n + 1) * TILE)
            turned = dot(res_hi[...], rot_hi[:, s]) + dot(res_hi[...], rot_lo[:, s]) + dot(res_lo[...], rot_hi[:, s])
            turned = turned.astype(BF16)
            for h, blk in enumerate(blocks):
                send2[pl.ds(blk * NL, NL), :, s] = turned[h * BLK : (h + 1) * BLK].reshape(NL, CAP, TILE)

        def give_back(there_p, there_l):
            pltpu.make_async_remote_copy(
                src_ref=send2.at[there_p * NL + there_l], dst_ref=recv2.at[me],
                send_sem=sem_send.at[1], recv_sem=sem_recv.at[1],
                device_id=(there_p, there_l), device_id_type=MESH,
            ).start()

        for core in range(2):
            for blk in blocks:
                for a in (2, 1, 3, 0):
                    for lo in (2 - 2 * at.y_lo, 2 * at.y_lo):
                        there_l = at.x_part[a] + lo + core
                        if a == 0 and blk is blocks[1]:

                            @pl.when((blk != p) | (there_l != l))
                            def _():
                                give_back(blk, there_l)
                        else:
                            give_back(blk, there_l)
        return 0

    lax.fori_loop(0, NP // 2, chunk, 0)
    pltpu.make_async_copy(send2.at[me], recv2.at[me], sem_recv.at[1]).start()

    whole(send1.at[pl.ds(0, DEV - 1)], sem_send.at[0])
    whole(id1_s.at[pl.ds(0, NP - 1)], sem_id.at[0])
    whole(id2_s.at[pl.ds(0, NL - 1)], sem_id.at[2])
    store_unpack.wait()
    store_cent.wait()
    whole(send2.at[pl.ds(0, DEV - 1)], sem_send.at[1])
    whole(recv2, sem_recv.at[1])


def finish(unpack, rows, cent, out, cent_out, buf, sem):
    store = pltpu.make_async_copy(cent, cent_out, sem.at[D // TILE])
    store.start()
    stores = []
    for n in range(D // TILE):
        s = pl.ds(n * TILE, TILE)
        buf[:, s] = dot(unpack[...], rows[:, :, s].reshape(DEV * CAP, TILE)).astype(BF16)
        stores.append(pltpu.make_async_copy(buf.at[:, s], out.at[:, s], sem.at[n]))
        stores[-1].start()
    for copy in (store, *stores):
        copy.wait()


def shards(passages, list_ids, old_centroids, rotation):
    vmem = pl.BlockSpec(memory_space=pltpu.VMEM)
    hbm = pl.BlockSpec(memory_space=pl.ANY)
    slots = jax.ShapeDtypeStruct((DEV, CAP, D), BF16)
    buffer = pltpu.VMEM((DEV, CAP, D), BF16)
    means = jax.ShapeDtypeStruct((LISTS, D), F32)
    arrays = (list_ids.reshape(1, ROWS), passages, old_centroids, rotation)
    rows, cent, unpack = pl.pallas_call(
        kernel,
        out_shape=(slots, means, jax.ShapeDtypeStruct((ROWS, DEV * CAP), BF16)),
        in_specs=[hbm] * 4,
        out_specs=(hbm,) * 3,
        scratch_shapes=[
            pltpu.VMEM((1, ROWS), I32),
            pltpu.VMEM((ROWS, D), BF16),
            pltpu.VMEM((LISTS, D), F32),
            pltpu.VMEM((D, D), F32),
            pltpu.VMEM((D, D), BF16),
            pltpu.VMEM((D, D), BF16),
            buffer, buffer, buffer,
            pltpu.VMEM((LISTS, D), F32),
            pltpu.VMEM((LISTS, D), BF16),
            pltpu.VMEM((LISTS, D), BF16),
            pltpu.VMEM((2 * BLK, D), BF16),
            pltpu.VMEM((2 * BLK, D), BF16),
            pltpu.VMEM((LISTS, DEV * CAP), BF16),
            pltpu.VMEM((DEV * CAP, LISTS), BF16),
            pltpu.VMEM((ROWS, DEV * CAP), BF16),
            pltpu.VMEM((NP, 1, BLK), I32),
            pltpu.VMEM((NP, 1, BLK), I32),
            pltpu.VMEM((NL, NP, BLK), I32),
            pltpu.VMEM((NL, NP, BLK), I32),
            pltpu.SemaphoreType.DMA((2,)),
            pltpu.SemaphoreType.DMA((2,)),
            pltpu.SemaphoreType.DMA((4,)),
            pltpu.SemaphoreType.DMA((4,)),
            pltpu.SemaphoreType.REGULAR,
        ],
        compiler_params=pltpu.CompilerParams(
            collective_id=0, has_side_effects=True, vmem_limit_bytes=36 << 20
        ),
        cost_estimate=pl.CostEstimate(flops=14 << 30, bytes_accessed=10 << 20, transcendentals=0),
    )(*(pltpu.with_memory_space_constraint(a, pltpu.HBM) for a in arrays))
    return pl.pallas_call(
        finish,
        out_shape=(jax.ShapeDtypeStruct((ROWS, D), BF16), means),
        in_specs=[vmem, vmem, hbm],
        out_specs=(hbm, hbm),
        scratch_shapes=[pltpu.VMEM((ROWS, D), BF16), pltpu.SemaphoreType.DMA((D // TILE + 1,))],
        compiler_params=pltpu.CompilerParams(vmem_limit_bytes=16 << 20),
        cost_estimate=pl.CostEstimate(flops=1 << 30, bytes_accessed=9 << 20, transcendentals=0),
    )(unpack, rows, cent)


def solution(mesh):
    split = P(("passage", "list"), None)
    return jax.shard_map(
        shards,
        mesh=mesh,
        in_specs=(split, P(("passage", "list")), split, P()),
        out_specs=(split, split),
        check_vma=False,
    )
```

time: 70.5 us -> 66.5 us (0.943)
  local copies, waits for them, and re-layouts: 4.19 us -> 0 us
    unnamed x6 -> x0, local copies, waits for them, and re-layouts: 4.19 us -> none
    pallas_call x1 -> x2, Pallas kernels: 65.4 us -> 65.8 us  [the longest x1 63.6 us: shards(): pl.pallas_call(kernel, out_shape=(slots, means, jax.ShapeDtypeStruct((ROW...]
where the time goes in v2:
time: 66.5 us; the launch traced here: 66.4 us
  Pallas kernels  65.8 us (99%)
    pallas_call x1, Pallas kernels, shards(): pl.pallas_call(kernel, out_shape=(slots, means, jax.ShapeDtypeStruct((ROW...  63.6 us
    pallas_call x1, Pallas kernels, shards(): pl.pallas_call(finish, out_shape=(jax.ShapeDtypeStruct((ROWS, D), BF16),...  2.14 us

profile of v2, /device:TPU:1, one launch (start us, length us, event | category | flops | bytes accessed | tf_op | source)
XLA Modules:
  0.0 66.4 jit_solution(13880220067140849335)
XLA Ops:
  0.6 63.6 %shard_map.59 = (bf16[128,8,1024]{2,1,0:T(8,128)(2,1)S(1)}, f32[512,1024]{1,0:T(8,128)S(1)}, bf16[512,1024]{1,0:T(8,128)(2,1)S(1)}) custom-call(s32[1,512]{1,0:T(1,128)} %bitcast.1, bf16[512,1024]{1,0:T(8,128)(2,1)} %pass_hbm.1, f32[512,1024]{1,0:T(8,128)} %old_hbm.1, f32[1024,1024]{1,0:T(8,128)} %rot_hbm.1), custom_call_target="tpu_custom_call" | custom-call | flops 15032385536 | bytes 10485760 | tf_op jit(solution)/shard_map/pallas_call | solution.py:302
  64.3 2.1 %shard_map.60 = (bf16[512,1024]{1,0:T(8,128)(2,1)}, f32[512,1024]{1,0:T(8,128)}) custom-call(bf16[512,1024]{1,0:T(8,128)(2,1)S(1)} %get-tuple-element.5.unpack, bf16[128,8,1024]{2,1,0:T(8,128)(2,1)S(1)} %get-tuple-element.6.rows, f32[512,1024]{1,0:T(8,128)S(1)} %get-tuple-element.7.cent), custom_call_target="tpu_custom_call" | custom-call | flops 1073741824 | bytes 9437184 | tf_op jit(solution)/shard_map/pallas_call | solution.py:338

commit v3 on v2

--- a/solution.py
+++ b/solution.py
@@ -1,3 +1,5 @@
+import random
+
 import jax
 import jax.numpy as jnp
 from jax import lax
@@ -13,6 +15,9 @@
 D = 1024
 BLK = NL * CAP
 TILE = 256
+PARTS = 4
+PACK = 512
+CHUNK = 32
 MESH = pl.DeviceIdType.MESH
 F32, BF16, I32 = jnp.float32, jnp.bfloat16, jnp.int32
 
@@ -33,8 +38,19 @@
     return sum(min(d, 4 - d) for d in offset)
 
 
-OFFSETS = sorted(((a, b, c) for a in range(4) for b in range(4) for c in range(4)), key=steps, reverse=True)
+def send_order(seed):
+    offsets = [(a, b, c) for a in range(4) for b in range(4) for c in range(4)]
+    random.Random(seed).shuffle(offsets)
+    return sorted(offsets, key=steps, reverse=True)
+
+
+OFFSETS = send_order(3)
+CHIPS = len(OFFSETS)
 HERE = (0, 0, 0)
+
+
+def seen_from_there(offset):
+    return OFFSETS.index(tuple((4 - d) % 4 for d in offset))
 
 
 class Place:
@@ -106,17 +122,20 @@
     load_pass.wait()
 
     def fill(b, _):
-        hit = slot_row == iota((BLK, ROWS), 0) + b * BLK
-        rows = dot(jnp.where(hit, 1.0, 0.0).astype(BF16), pass_ref[...])
-        send1[pl.ds(b * NL, NL)] = rows.astype(BF16).reshape(NL, CAP, D)
+        hit = slot_row == iota((PACK, ROWS), 0) + b * PACK
+        hit = jnp.where(hit, 1.0, 0.0).astype(BF16)
+        at_b = pl.ds(b * (PACK // CAP), PACK // CAP)
+        for n in range(D // TILE):
+            cols = slice(n * TILE, (n + 1) * TILE)
+            send1[at_b, :, cols] = dot(hit, pass_ref[:, cols]).astype(BF16).reshape(PACK // CAP, CAP, TILE)
         return 0
 
-    lax.fori_loop(0, NP, fill, 0)
+    lax.fori_loop(0, DEV * CAP // PACK, fill, 0)
 
     def route(offset, core):
         device = at.at(offset, core)
         pltpu.make_async_remote_copy(
-            src_ref=send1.at[device[0] * NL + device[1]], dst_ref=recv1.at[me],
+            src_ref=send1.at[device[0] * NL + device[1]], dst_ref=recv1.at[at.core * CHIPS + seen_from_there(offset)],
             send_sem=sem_send.at[0], recv_sem=sem_recv.at[0], device_id=device, device_id_type=MESH,
         ).start()
 
@@ -129,7 +148,7 @@
         for core in range(2):
             route(offset, core)
     route(HERE, 1 - at.core)
-    pltpu.make_async_copy(send1.at[me], recv1.at[me], sem_recv.at[0]).start()
+    pltpu.make_async_copy(send1.at[me], recv1.at[at.core * CHIPS + OFFSETS.index(HERE)], sem_recv.at[0]).start()
 
     before_col = jnp.sum(jnp.where(own_row < own_col, 1.0, 0.0), axis=1, keepdims=True)
     slot_col = (own_col * CAP + iota((ROWS, 1), 0).astype(F32) - before_col).astype(I32)
@@ -165,11 +184,13 @@
     route_all(0)
 
     whole(id1_r, sem_id.at[1])
-    lane = iota((NP, BLK), 1)
-    mine = (lane >= l * CAP) & (lane < l * CAP + CAP)
+    source = iota((NP, BLK), 1) // CAP
     got = id1_r[...].reshape(NP, BLK)
     for k in range(NL):
-        id2_s[k] = jnp.where(mine, pltpu.roll(got, CAP * wrap(l - k + NL, NL), 1), 0)
+        spread = jnp.where(source == k, got, 0)
+        for turn in (CAP, 2 * CAP, 4 * CAP, 8 * CAP):
+            spread = spread + pltpu.roll(spread, turn, 1)
+        id2_s[k] = spread
     for k in range(1, NL):
         other = wrap(l + k, NL)
         pltpu.make_async_remote_copy(
@@ -193,11 +214,21 @@
     lax.fori_loop(0, D // 128, split_rot, 0)
 
     whole(id2_r, sem_id.at[3])
-    marks = jnp.sum(id2_r[...].astype(F32), axis=0)
+    row_of = jnp.zeros((CHIPS, 1), I32)
+    for k, offset in enumerate(OFFSETS):
+        there_p, there_l = at.at(offset, 0)
+        row_of = jnp.where(iota((CHIPS, 1), 0) == k, there_l * NP + there_p, row_of)
+    here = iota((CHIPS, DEV), 1)
+    order = jnp.concatenate([here == row_of, here == row_of + NP], axis=0)
+    order = jnp.where(order, 1.0, 0.0).astype(BF16)
+    marks = id2_r[...].reshape(DEV, BLK).astype(F32)
+    high = jnp.floor(marks * (1.0 / 16))
+    marks = dot(order, high.astype(BF16)) * 16.0 + dot(order, (marks - high * 16.0).astype(BF16))
+    marks = jnp.where(iota((DEV, BLK), 0) % NL == iota((DEV, BLK), 1) // CAP, marks, 0.0)
     eye = iota((BLK, BLK), 0) == iota((BLK, BLK), 1)
     tally = jnp.zeros((LISTS, 1), F32)
     for b in range(NP):
-        row = marks[b : b + 1, :]
+        row = jnp.sum(marks[b * NL : (b + 1) * NL, :], axis=0, keepdims=True)
         hit = jnp.where(iota((LISTS, BLK), 0) + 1 == row.astype(I32), 1.0, 0.0)
         member[:, b * BLK : (b + 1) * BLK] = hit.astype(BF16)
         tally = tally + jnp.sum(hit, axis=1, keepdims=True)
@@ -219,56 +250,37 @@
     store_cent = pltpu.make_async_copy(cent, cent_out, sem_local.at[1])
     store_cent.start()
 
-    def chunk(i, _):
-        far = lax.div(i, 2)
-        flip = i - 2 * far
-        y_hi = wrap(at.y_hi + 1 + far, 2)
-        y_hi = wrap(y_hi, 2)
-        z_a = wrap(at.z_part[0] + 2 + flip, 4)
-        z_b = wrap(at.z_part[0] + 1 + 3 * flip, 4)
-        z_b = wrap(z_b, 4)
-        blocks = (y_hi * 4 + z_a, y_hi * 4 + z_b)
-        for h, blk in enumerate(blocks):
-            half = slice(h * BLK, (h + 1) * BLK)
-            pick = member_t[pl.ds(pl.multiple_of(blk * BLK, BLK), BLK), :]
-            for n in range(D // TILE):
-                s = slice(n * TILE, (n + 1) * TILE)
-                near = dot(pick, cent_hi[:, s]) + dot(pick, cent_lo[:, s])
-                rows = recv1[pl.ds(blk * NL, NL), :, s].reshape(BLK, TILE).astype(F32)
-                res = rows - near
-                high = res.astype(BF16)
-                res_hi[half, s] = high
-                res_lo[half, s] = (res - high.astype(F32)).astype(BF16)
+    for first in range(0, DEV, CHUNK):
+        here = slice(first, first + CHUNK)
+        pick = member_t[first * CAP : (first + CHUNK) * CAP, :]
+        for n in range(D // TILE):
+            s = slice(n * TILE, (n + 1) * TILE)
+            near = dot(pick, cent_hi[:, s]) + dot(pick, cent_lo[:, s])
+            res = recv1[here, :, s].reshape(CHUNK * CAP, TILE).astype(F32) - near
+            high = res.astype(BF16)
+            res_hi[:, s] = high
+            res_lo[:, s] = (res - high.astype(F32)).astype(BF16)
         for n in range(D // TILE):
             s = slice(n * TILE, (n + 1) * TILE)
             turned = dot(res_hi[...], rot_hi[:, s]) + dot(res_hi[...], rot_lo[:, s]) + dot(res_lo[...], rot_hi[:, s])
-            turned = turned.astype(BF16)
-            for h, blk in enumerate(blocks):
-                send2[pl.ds(blk * NL, NL), :, s] = turned[h * BLK : (h + 1) * BLK].reshape(NL, CAP, TILE)
-
-        def give_back(there_p, there_l):
-            pltpu.make_async_remote_copy(
-                src_ref=send2.at[there_p * NL + there_l], dst_ref=recv2.at[me],
-                send_sem=sem_send.at[1], recv_sem=sem_recv.at[1],
-                device_id=(there_p, there_l), device_id_type=MESH,
-            ).start()
-
-        for core in range(2):
-            for blk in blocks:
-                for a in (2, 1, 3, 0):
-                    for lo in (2 - 2 * at.y_lo, 2 * at.y_lo):
-                        there_l = at.x_part[a] + lo + core
-                        if a == 0 and blk is blocks[1]:
-
-                            @pl.when((blk != p) | (there_l != l))
-                            def _():
-                                give_back(blk, there_l)
-                        else:
-                            give_back(blk, there_l)
-        return 0
-
-    lax.fori_loop(0, NP // 2, chunk, 0)
-    pltpu.make_async_copy(send2.at[me], recv2.at[me], sem_recv.at[1]).start()
+            send2[here, :, s] = turned.astype(BF16).reshape(CHUNK, CAP, TILE)
+
+        for k in range(first, first + CHUNK):
+            core, offset = k // CHIPS, OFFSETS[k % CHIPS]
+
+            def give_back():
+                pltpu.make_async_remote_copy(
+                    src_ref=send2.at[k], dst_ref=recv2.at[me], send_sem=sem_send.at[1], recv_sem=sem_recv.at[1],
+                    device_id=at.at(offset, core), device_id_type=MESH,
+                ).start()
+
+            if offset == HERE:
+                pl.when(at.core != core)(give_back)
+            else:
+                give_back()
+
+    mine = send2.at[at.core * CHIPS + OFFSETS.index(HERE)]
+    pltpu.make_async_copy(mine, recv2.at[me], sem_recv.at[1]).start()
 
     whole(send1.at[pl.ds(0, DEV - 1)], sem_send.at[0])
     whole(id1_s.at[pl.ds(0, NP - 1)], sem_id.at[0])
@@ -280,15 +292,20 @@
 
 
 def finish(unpack, rows, cent, out, cent_out, buf, sem):
-    store = pltpu.make_async_copy(cent, cent_out, sem.at[D // TILE])
-    store.start()
     stores = []
-    for n in range(D // TILE):
-        s = pl.ds(n * TILE, TILE)
-        buf[:, s] = dot(unpack[...], rows[:, :, s].reshape(DEV * CAP, TILE)).astype(BF16)
-        stores.append(pltpu.make_async_copy(buf.at[:, s], out.at[:, s], sem.at[n]))
+
+    def store(src, dst):
+        stores.append(pltpu.make_async_copy(src, dst, sem.at[len(stores)]))
         stores[-1].start()
-    for copy in (store, *stores):
+
+    for n in range(PARTS):
+        rows_n = pl.ds(n * (LISTS // PARTS), LISTS // PARTS)
+        store(cent.at[rows_n], cent_out.at[rows_n])
+    for n in range(PARTS):
+        rows_n = pl.ds(n * (ROWS // PARTS), ROWS // PARTS)
+        buf[rows_n] = dot(unpack[rows_n], rows[...].reshape(DEV * CAP, D)).astype(BF16)
+        store(buf.at[rows_n], out.at[rows_n])
+    for copy in stores:
         copy.wait()
 
 
@@ -315,8 +332,8 @@
             pltpu.VMEM((LISTS, D), F32),
             pltpu.VMEM((LISTS, D), BF16),
             pltpu.VMEM((LISTS, D), BF16),
-            pltpu.VMEM((2 * BLK, D), BF16),
-            pltpu.VMEM((2 * BLK, D), BF16),
+            pltpu.VMEM((CHUNK * CAP, D), BF16),
+            pltpu.VMEM((CHUNK * CAP, D), BF16),
             pltpu.VMEM((LISTS, DEV * CAP), BF16),
             pltpu.VMEM((DEV * CAP, LISTS), BF16),
             pltpu.VMEM((ROWS, DEV * CAP), BF16),
@@ -340,7 +357,7 @@
         out_shape=(jax.ShapeDtypeStruct((ROWS, D), BF16), means),
         in_specs=[vmem, vmem, hbm],
         out_specs=(hbm, hbm),
-        scratch_shapes=[pltpu.VMEM((ROWS, D), BF16), pltpu.SemaphoreType.DMA((D // TILE + 1,))],
+        scratch_shapes=[pltpu.VMEM((ROWS, D), BF16), pltpu.SemaphoreType.DMA((2 * PARTS,))],
         compiler_params=pltpu.CompilerParams(vmem_limit_bytes=16 << 20),
         cost_estimate=pl.CostEstimate(flops=1 << 30, bytes_accessed=9 << 20, transcendentals=0),
     )(unpack, rows, cent)

time: 66.5 us -> 62.9 us (0.946)
  Pallas kernels: 65.8 us -> 62 us
    pallas_call x1, Pallas kernels: 63.6 us -> 60 us  [shards(): pl.pallas_call(kernel, out_shape=(slots, means, jax.ShapeDtypeStruct((ROW...]
where the time goes in v3:
time: 62.9 us; the launch traced here: 62.8 us
  Pallas kernels  62 us (99%)
  between operations  0.8 us (1%)
    pallas_call x1, Pallas kernels, shards(): pl.pallas_call(kernel, out_shape=(slots, means, jax.ShapeDtypeStruct((ROW...  60 us
    pallas_call x1, Pallas kernels, shards(): pl.pallas_call(finish, out_shape=(jax.ShapeDtypeStruct((ROWS, D), BF16),...  2.05 us

profile of v3, /device:TPU:1, one launch (start us, length us, event | category | flops | bytes accessed | tf_op | source)
XLA Modules:
  0.0 62.8 jit_solution(13431765635971654201)
XLA Ops:
  0.6 60.0 %shard_map.59 = (bf16[128,8,1024]{2,1,0:T(8,128)(2,1)S(1)}, f32[512,1024]{1,0:T(8,128)S(1)}, bf16[512,1024]{1,0:T(8,128)(2,1)S(1)}) custom-call(s32[1,512]{1,0:T(1,128)} %bitcast.1, bf16[512,1024]{1,0:T(8,128)(2,1)} %pass_hbm.1, f32[512,1024]{1,0:T(8,128)} %old_hbm.1, f32[1024,1024]{1,0:T(8,128)} %rot_hbm.1), custom_call_target="tpu_custom_call" | custom-call | flops 15032385536 | bytes 10485760 | tf_op jit(solution)/shard_map/pallas_call | solution.py:319
  60.6 2.0 %shard_map.60 = (bf16[512,1024]{1,0:T(8,128)(2,1)}, f32[512,1024]{1,0:T(8,128)}) custom-call(bf16[512,1024]{1,0:T(8,128)(2,1)S(1)} %get-tuple-element.5.unpack, bf16[128,8,1024]{2,1,0:T(8,128)(2,1)S(1)} %get-tuple-element.6.rows, f32[512,1024]{1,0:T(8,128)S(1)} %get-tuple-element.7.cent), custom_call_target="tpu_custom_call" | custom-call | flops 1073741824 | bytes 9437184 | tf_op jit(solution)/shard_map/pallas_call | solution.py:355

commit v4 on v3

--- a/solution.py
+++ b/solution.py
@@ -17,7 +17,8 @@
 TILE = 256
 PARTS = 4
 PACK = 512
-CHUNK = 32
+CHUNKS = (16, 16, 32, 32, 32)
+WIDE = 256
 MESH = pl.DeviceIdType.MESH
 F32, BF16, I32 = jnp.float32, jnp.bfloat16, jnp.int32
 
@@ -84,7 +85,7 @@
 def kernel(
     ids_hbm, pass_hbm, old_hbm, rot_hbm, recv2, cent_out, unpack_out,
     ids_ref, pass_ref, old, rot, rot_hi, rot_lo, send1, recv1, send2,
-    cent, cent_hi, cent_lo, res_hi, res_lo, member, member_t, unpack,
+    cent, cent_hi, cent_lo, res, member, member_t, unpack,
     id1_s, id1_r, id2_s, id2_r,
     sem_send, sem_recv, sem_id, sem_local, sem_bar,
 ):
@@ -250,22 +251,25 @@
     store_cent = pltpu.make_async_copy(cent, cent_out, sem_local.at[1])
     store_cent.start()
 
-    for first in range(0, DEV, CHUNK):
-        here = slice(first, first + CHUNK)
-        pick = member_t[first * CAP : (first + CHUNK) * CAP, :]
-        for n in range(D // TILE):
-            s = slice(n * TILE, (n + 1) * TILE)
+    first = 0
+    for count in CHUNKS:
+        here = slice(first, first + count)
+        rows = count * CAP
+        pick = member_t[first * CAP : first * CAP + rows, :]
+        for n in range(D // WIDE):
+            s = slice(n * WIDE, (n + 1) * WIDE)
             near = dot(pick, cent_hi[:, s]) + dot(pick, cent_lo[:, s])
-            res = recv1[here, :, s].reshape(CHUNK * CAP, TILE).astype(F32) - near
-            high = res.astype(BF16)
-            res_hi[:, s] = high
-            res_lo[:, s] = (res - high.astype(F32)).astype(BF16)
-        for n in range(D // TILE):
-            s = slice(n * TILE, (n + 1) * TILE)
-            turned = dot(res_hi[...], rot_hi[:, s]) + dot(res_hi[...], rot_lo[:, s]) + dot(res_lo[...], rot_hi[:, s])
-            send2[here, :, s] = turned.astype(BF16).reshape(CHUNK, CAP, TILE)
-
-        for k in range(first, first + CHUNK):
+            part = recv1[here, :, s].reshape(rows, WIDE).astype(F32) - near
+            high = part.astype(BF16)
+            res[:rows, s] = high
+            res[rows : 2 * rows, s] = (part - high.astype(F32)).astype(BF16)
+        for n in range(D // WIDE):
+            s = slice(n * WIDE, (n + 1) * WIDE)
+            both = dot(res[: 2 * rows], rot_hi[:, s])
+            turned = both[:rows] + both[rows:] + dot(res[:rows], rot_lo[:, s])
+            send2[here, :, s] = turned.astype(BF16).reshape(count, CAP, WIDE)
+
+        for k in range(first, first + count):
             core, offset = k // CHIPS, OFFSETS[k % CHIPS]
 
             def give_back():
@@ -278,6 +282,7 @@
                 pl.when(at.core != core)(give_back)
             else:
                 give_back()
+        first += count
 
     mine = send2.at[at.core * CHIPS + OFFSETS.index(HERE)]
     pltpu.make_async_copy(mine, recv2.at[me], sem_recv.at[1]).start()
@@ -332,8 +337,7 @@
             pltpu.VMEM((LISTS, D), F32),
             pltpu.VMEM((LISTS, D), BF16),
             pltpu.VMEM((LISTS, D), BF16),
-            pltpu.VMEM((CHUNK * CAP, D), BF16),
-            pltpu.VMEM((CHUNK * CAP, D), BF16),
+            pltpu.VMEM((2 * max(CHUNKS) * CAP, D), BF16),
             pltpu.VMEM((LISTS, DEV * CAP), BF16),
             pltpu.VMEM((DEV * CAP, LISTS), BF16),
             pltpu.VMEM((ROWS, DEV * CAP), BF16),

time: 62.9 us -> 62.2 us (0.989)
  Pallas kernels: 62 us -> 61.3 us
    pallas_call x1, Pallas kernels: 60 us -> 59.3 us  [shards(): pl.pallas_call(kernel, out_shape=(slots, means, jax.ShapeDtypeStruct((ROW...]
where the time goes in v4:
time: 62.2 us; the launch traced here: 62.1 us
  Pallas kernels  61.3 us (99%)
  between operations  0.8 us (1%)
    pallas_call x1, Pallas kernels, shards(): pl.pallas_call(kernel, out_shape=(slots, means, jax.ShapeDtypeStruct((ROW...  59.3 us
    pallas_call x1, Pallas kernels, shards(): pl.pallas_call(finish, out_shape=(jax.ShapeDtypeStruct((ROWS, D), BF16),...  2.05 us

profile of v4, /device:TPU:1, one launch (start us, length us, event | category | flops | bytes accessed | tf_op | source)
XLA Modules:
  0.0 62.1 jit_solution(9632103271175048307)
XLA Ops:
  0.6 59.3 %shard_map.59 = (bf16[128,8,1024]{2,1,0:T(8,128)(2,1)S(1)}, f32[512,1024]{1,0:T(8,128)S(1)}, bf16[512,1024]{1,0:T(8,128)(2,1)S(1)}) custom-call(s32[1,512]{1,0:T(1,128)} %bitcast.1, bf16[512,1024]{1,0:T(8,128)(2,1)} %pass_hbm.1, f32[512,1024]{1,0:T(8,128)} %old_hbm.1, f32[1024,1024]{1,0:T(8,128)} %rot_hbm.1), custom_call_target="tpu_custom_call" | custom-call | flops 15032385536 | bytes 10485760 | tf_op jit(solution)/shard_map/pallas_call | solution.py:324
  59.9 2.1 %shard_map.60 = (bf16[512,1024]{1,0:T(8,128)(2,1)}, f32[512,1024]{1,0:T(8,128)}) custom-call(bf16[512,1024]{1,0:T(8,128)(2,1)S(1)} %get-tuple-element.5.unpack, bf16[128,8,1024]{2,1,0:T(8,128)(2,1)S(1)} %get-tuple-element.6.rows, f32[512,1024]{1,0:T(8,128)S(1)} %get-tuple-element.7.cent), custom_call_target="tpu_custom_call" | custom-call | flops 1073741824 | bytes 9437184 | tf_op jit(solution)/shard_map/pallas_call | solution.py:359

commit v5 on v4

--- a/solution.py
+++ b/solution.py
@@ -136,7 +136,7 @@
     def route(offset, core):
         device = at.at(offset, core)
         pltpu.make_async_remote_copy(
-            src_ref=send1.at[device[0] * NL + device[1]], dst_ref=recv1.at[at.core * CHIPS + seen_from_there(offset)],
+            src_ref=send1.at[device[0] * NL + device[1]], dst_ref=recv1.at[(1 - at.core) * CHIPS + seen_from_there(offset)],
             send_sem=sem_send.at[0], recv_sem=sem_recv.at[0], device_id=device, device_id_type=MESH,
         ).start()
 
@@ -149,7 +149,7 @@
         for core in range(2):
             route(offset, core)
     route(HERE, 1 - at.core)
-    pltpu.make_async_copy(send1.at[me], recv1.at[at.core * CHIPS + OFFSETS.index(HERE)], sem_recv.at[0]).start()
+    pltpu.make_async_copy(send1.at[me], recv1.at[(1 - at.core) * CHIPS + OFFSETS.index(HERE)], sem_recv.at[0]).start()
 
     before_col = jnp.sum(jnp.where(own_row < own_col, 1.0, 0.0), axis=1, keepdims=True)
     slot_col = (own_col * CAP + iota((ROWS, 1), 0).astype(F32) - before_col).astype(I32)
@@ -220,7 +220,7 @@
         there_p, there_l = at.at(offset, 0)
         row_of = jnp.where(iota((CHIPS, 1), 0) == k, there_l * NP + there_p, row_of)
     here = iota((CHIPS, DEV), 1)
-    order = jnp.concatenate([here == row_of, here == row_of + NP], axis=0)
+    order = jnp.concatenate([here == row_of + NP, here == row_of], axis=0)
     order = jnp.where(order, 1.0, 0.0).astype(BF16)
     marks = id2_r[...].reshape(DEV, BLK).astype(F32)
     high = jnp.floor(marks * (1.0 / 16))
@@ -270,7 +270,7 @@
             send2[here, :, s] = turned.astype(BF16).reshape(count, CAP, WIDE)
 
         for k in range(first, first + count):
-            core, offset = k // CHIPS, OFFSETS[k % CHIPS]
+            core, offset = 1 - k // CHIPS, OFFSETS[k % CHIPS]
 
             def give_back():
                 pltpu.make_async_remote_copy(
@@ -284,7 +284,7 @@
                 give_back()
         first += count
 
-    mine = send2.at[at.core * CHIPS + OFFSETS.index(HERE)]
+    mine = send2.at[(1 - at.core) * CHIPS + OFFSETS.index(HERE)]
     pltpu.make_async_copy(mine, recv2.at[me], sem_recv.at[1]).start()
 
     whole(send1.at[pl.ds(0, DEV - 1)], sem_send.at[0])

time: 62.2 us -> 61.5 us (0.989)
  the two profiles are of different devices: /device:TPU:1 before, /device:TPU:0 now
where the time goes in v5:
time: 61.5 us; the launch traced here: 61.4 us
  Pallas kernels  60.6 us (99%)
  between operations  0.8 us (1%)
    pallas_call x1, Pallas kernels, shards(): pl.pallas_call(kernel, out_shape=(slots, means, jax.ShapeDtypeStruct((ROW...  58.6 us
    pallas_call x1, Pallas kernels, shards(): pl.pallas_call(finish, out_shape=(jax.ShapeDtypeStruct((ROWS, D), BF16),...  2.04 us

profile of v5, /device:TPU:0, one launch (start us, length us, event | category | flops | bytes accessed | tf_op | source)
XLA Modules:
  0.0 61.4 jit_solution(15012672980919987191)
XLA Ops:
  0.6 58.6 %shard_map.59 = (bf16[128,8,1024]{2,1,0:T(8,128)(2,1)S(1)}, f32[512,1024]{1,0:T(8,128)S(1)}, bf16[512,1024]{1,0:T(8,128)(2,1)S(1)}) custom-call(s32[1,512]{1,0:T(1,128)} %bitcast.1, bf16[512,1024]{1,0:T(8,128)(2,1)} %pass_hbm.1, f32[512,1024]{1,0:T(8,128)} %old_hbm.1, f32[1024,1024]{1,0:T(8,128)} %rot_hbm.1), custom_call_target="tpu_custom_call" | custom-call | flops 15032385536 | bytes 10485760 | tf_op jit(solution)/shard_map/pallas_call | solution.py:324
  59.2 2.0 %shard_map.60 = (bf16[512,1024]{1,0:T(8,128)(2,1)}, f32[512,1024]{1,0:T(8,128)}) custom-call(bf16[512,1024]{1,0:T(8,128)(2,1)S(1)} %get-tuple-element.5.unpack, bf16[128,8,1024]{2,1,0:T(8,128)(2,1)S(1)} %get-tuple-element.6.rows, f32[512,1024]{1,0:T(8,128)S(1)} %get-tuple-element.7.cent), custom_call_target="tpu_custom_call" | custom-call | flops 1073741824 | bytes 9437184 | tf_op jit(solution)/shard_map/pallas_call | solution.py:359

commit v6 on v5

--- a/solution.py
+++ b/solution.py
@@ -17,8 +17,8 @@
 TILE = 256
 PARTS = 4
 PACK = 512
-CHUNKS = (16, 16, 32, 32, 32)
-WIDE = 256
+CHUNKS = (16, 16, 32, 32, 16, 16)
+WIDE = 512
 MESH = pl.DeviceIdType.MESH
 F32, BF16, I32 = jnp.float32, jnp.bfloat16, jnp.int32
 

time: 61.5 us -> 61.5 us (level)
  no operation moved by 1% of the time
where the time goes in v6:
time: 61.5 us; the launch traced here: 61.4 us
  Pallas kernels  60.6 us (99%)
  between operations  0.8 us (1%)
    pallas_call x1, Pallas kernels, shards(): pl.pallas_call(kernel, out_shape=(slots, means, jax.ShapeDtypeStruct((ROW...  58.6 us
    pallas_call x1, Pallas kernels, shards(): pl.pallas_call(finish, out_shape=(jax.ShapeDtypeStruct((ROWS, D), BF16),...  2.04 us

profile of v6, /device:TPU:0, one launch (start us, length us, event | category | flops | bytes accessed | tf_op | source)
XLA Modules:
  0.0 61.4 jit_solution(9540846952731129392)
XLA Ops:
  0.6 58.6 %shard_map.59 = (bf16[128,8,1024]{2,1,0:T(8,128)(2,1)S(1)}, f32[512,1024]{1,0:T(8,128)S(1)}, bf16[512,1024]{1,0:T(8,128)(2,1)S(1)}) custom-call(s32[1,512]{1,0:T(1,128)} %bitcast.1, bf16[512,1024]{1,0:T(8,128)(2,1)} %pass_hbm.1, f32[512,1024]{1,0:T(8,128)} %old_hbm.1, f32[1024,1024]{1,0:T(8,128)} %rot_hbm.1), custom_call_target="tpu_custom_call" | custom-call | flops 15032385536 | bytes 10485760 | tf_op jit(solution)/shard_map/pallas_call | solution.py:324
  59.2 2.0 %shard_map.60 = (bf16[512,1024]{1,0:T(8,128)(2,1)}, f32[512,1024]{1,0:T(8,128)}) custom-call(bf16[512,1024]{1,0:T(8,128)(2,1)S(1)} %get-tuple-element.5.unpack, bf16[128,8,1024]{2,1,0:T(8,128)(2,1)S(1)} %get-tuple-element.6.rows, f32[512,1024]{1,0:T(8,128)S(1)} %get-tuple-element.7.cent), custom_call_target="tpu_custom_call" | custom-call | flops 1073741824 | bytes 9437184 | tf_op jit(solution)/shard_map/pallas_call | solution.py:359
